TPU v7x, 256 devices: a whole 4x4x8 slice. The times are simulated.
256 devices in a mesh: gx: 8 (over y, core), gy: 32 (over x, z).
Axes of the slice: x: 4, y: 4, z: 8, core: 2. Of those that a mesh axis runs over, the one named last changes fastest.
Arguments:
- field: bfloat16 [1024, 256, 512], P('gx', 'gy'), may hold values from -6 to 6
- conv_weight: bfloat16 [27, 32, 32], replicated, may hold values from -0.21875 to 0.21875
- conv_bias: float32 [32], replicated, may hold values from -3 to 3
- spectral_weight: bfloat16 [32, 2, 32, 32], replicated, may hold values from -2 to 2
Outputs:
- layer_out: bfloat16 [1024, 256, 512], P('gx', 'gy')
All inputs are finite; a program needn't handle non-finite values.
Results may differ from a plain program's by a relative error of at most 0.0049.
Values may be sent and summed in bfloat16 or wider, within the bound.
A program may use at most 128 MiB of HBM per device.

v0:
```python
import math

import jax
import jax.numpy as jnp
from jax import lax
from jax.sharding import PartitionSpec as P


def extended(cells, sides, width):
    for axis, dim in sides:
        count = lax.axis_size(axis)
        ends = count - 1
        head = lax.slice_in_dim(cells, 0, width, axis=dim)
        tail = lax.slice_in_dim(cells, cells.shape[dim] - width, cells.shape[dim], axis=dim)
        cells = jnp.concatenate(
            [
                lax.ppermute(tail, axis, [(i, (i + 1) % count) for i in range(ends)]),
                cells,
                lax.ppermute(head, axis, [((i + 1) % count, i) for i in range(ends)]),
            ],
            axis=dim,
        )
    return cells


def make_tables(length, mode_count, first, count):
    positions = first + jnp.arange(count, dtype=jnp.int32)
    mode_ids = jnp.arange(mode_count, dtype=jnp.int32)
    turns = mode_ids[:, None] * positions[None, :] % length
    angles = turns.astype(jnp.float32) * (2.0 * math.pi / length)
    normalizer = 1.0 / math.sqrt(length)
    pairs = jnp.stack([jnp.cos(angles), -jnp.sin(angles)], axis=1) * normalizer
    doubling = jnp.where(mode_ids == 0, 1.0, 2.0).astype(jnp.float32)
    forward_table = pairs.reshape(2 * mode_count, count).astype(jnp.bfloat16)
    inverse_table = (
        (pairs * doubling[:, None, None]).reshape(2 * mode_count, count).T.astype(jnp.bfloat16)
    )
    return (forward_table, inverse_table)


def mixing_kernel(spectral_weight):
    real_part = spectral_weight[:, 0]
    imag_part = spectral_weight[:, 1]
    upper = jnp.stack([real_part, imag_part], axis=1)
    lower = jnp.stack([-imag_part, real_part], axis=1)
    return jnp.stack([upper, lower], axis=1)


def band_kernels(conv_weight, depth, channels):
    taps = conv_weight.reshape(3, 3, 3, channels, channels)
    inner = jnp.arange(depth, dtype=jnp.int32)
    offsets = jnp.arange(3, dtype=jnp.int32)
    shifts = inner[None, :, None] == inner[None, None, :] + offsets[:, None, None] - 1
    shifts = shifts.astype(jnp.bfloat16)
    bands = jnp.einsum("kzw,abkco->abzcwo", shifts, taps, preferred_element_type=jnp.float32)
    return bands.astype(jnp.bfloat16).reshape(3, 3, depth * channels, depth * channels)


def mix_modes(coef_rows, kernel_part):
    mode_count = kernel_part.shape[0]
    channels = kernel_part.shape[-1]
    total_width = coef_rows.shape[1]
    grouped = coef_rows.reshape(mode_count, 2, -1, channels)
    mixed = jnp.einsum(
        "mrpc,mrqco->mqpo", grouped, kernel_part, preferred_element_type=jnp.float32
    ).astype(jnp.bfloat16)
    return mixed.reshape(2 * mode_count, total_width)


def shards(field, conv_weight, conv_bias, spectral_weight):
    cells_x, cells_y, width = field.shape
    channels = conv_weight.shape[1]
    depth = width // channels
    mode_count = spectral_weight.shape[0]
    groups = lax.axis_size("gx")
    length = cells_x * groups
    padded = extended(field, (("gx", 0), ("gy", 1)), 1)
    bands = band_kernels(conv_weight, depth, channels)
    conv = jnp.zeros((cells_x * cells_y, width), jnp.float32)
    for step_x in range(3):
        for step_y in range(3):
            window = padded[step_x : step_x + cells_x, step_y : step_y + cells_y].reshape(
                cells_x * cells_y, width
            )
            conv = conv + jnp.dot(window, bands[step_x, step_y], preferred_element_type=jnp.float32)
    conv = conv.reshape(cells_x, cells_y, width)
    first_x = lax.axis_index("gx") * cells_x
    forward_table, inverse_table = make_tables(length, mode_count, first_x, cells_x)
    columns = field.reshape(cells_x, cells_y * width)
    kernel = mixing_kernel(spectral_weight)
    partial_value = jnp.dot(forward_table, columns, preferred_element_type=jnp.float32)
    coef = lax.psum(partial_value, "gx").astype(jnp.bfloat16)
    mixed = mix_modes(coef, kernel)
    spectral = jnp.dot(inverse_table, mixed, preferred_element_type=jnp.float32)
    combined = conv + spectral.reshape(cells_x, cells_y, width) + jnp.tile(conv_bias, depth)
    return jax.nn.gelu(combined, approximate=False).astype(jnp.bfloat16)


def solution(mesh):
    placed = (P("gx", "gy", None), P(), P(), P())
    return jax.shard_map(
        shards, mesh=mesh, in_specs=placed, out_specs=P("gx", "gy", None), check_vma=False
    )
```

profile of v0, /device:TPU:6, one launch (start us, length us, event | category | flops | bytes accessed | tf_op | source)
XLA Modules:
  0.0 145.4 jit_solution(12894187382482745172)
XLA Ops:
  0.0 0.7 fusion.94
  0.7 1.3 collective-permute-start.1
  2.0 3.0 %collective-permute-start = (bf16[1,8,512]{2,1,0:T(8,128)(2,1)S(1)}, bf16[1,8,512]{2,1,0:T(8,128)(2,1)S(1)}, u32[]{:S(2)}, u32[]{:S(2)}) collective-permute-start(bf16[1,8,512]{2,1,0:T(8,128)(2,1)S(1)} %get-tuple-element.7), channel_id=1, source_target_pairs={{0,32},{32,64},{64,96},{96,128},{128,160},{160,192},{192,224},{1,3... | collective-permute-start | bytes 24584 | tf_op jit(solution)/shard_map/ppermute | solution.py:17
  5.1 6.8 %convert_bitcast_fusion = bf16[3,3,16,32,16,32]{5,4,3,1,0,2:T(8,128)(2,1)S(1)} fusion(bf16[3,3,3,32,32]{4,3,2,1,0:T(8,128)(2,1)} %bitcast.128, s32[3,16]{1,0:T(4,128)S(1)} %add_add_fusion), kind=kOutput, calls=%fused_computation | convolution fusion | flops 16515840 | bytes 4774080 | tf_op jit(solution)/shard_map/kzw,abkco->abzcwo/dot_general | solution.py:55
  11.9 6.9 %copy.73 = bf16[3,3,16,32,16,32]{5,4,3,2,1,0:T(8,128)(2,1)} copy(bf16[3,3,16,32,16,32]{5,4,3,1,0,2:T(8,128)(2,1)S(1)} %convert_bitcast_fusion) | data formatting | bytes 9437184 | tf_op jit(solution)/shard_map/convert_element_type | solution.py:56
  18.8 25.3 %reshape.184 = bf16[3,3,512,512]{3,2,1,0:T(8,128)(2,1)} reshape(bf16[3,3,16,32,16,32]{5,4,3,2,1,0:T(8,128)(2,1)} %copy.73) | data formatting | bytes 9437184 | tf_op jit(solution)/shard_map/reshape | solution.py:56
  44.1 1.7 %fusion.64 = f32[512,1024]{0,1:T(8,128)S(1)} fusion(bf16[128,8,512]{2,1,0:T(8,128)(2,1)S(1)} %copy-done, bf16[3,3,512,512]{3,2,1,0:T(8,128)(2,1)} %reshape.184), kind=kOutput, calls=%fused_computation.72 | convolution fusion | flops 536870912 | bytes 3670016 | tf_op jit(solution)/shard_map/dot_general | solution.py:85
  46.0 0.4 copy.94
  46.4 1.3 fusion.95
  47.6 53.2 %all-reduce.1 = bf16[64,4096]{1,0:T(8,128)(2,1)} all-reduce(f32[64,4096]{1,0:T(8,128)} %fusion.95), channel_id=1, replica_groups=mesh['gx'=8,'gy'=32] {'gx'}, use_global_device_ids=true, to_apply=%region_0.1 | all-reduce | flops 262144 | bytes 1572864 | tf_op jit(solution)/shard_map/psum | solution.py:92
  100.8 3.5 %reshape.195 = bf16[32,2,128,32]{3,2,1,0:T(8,128)(2,1)} reshape(bf16[64,4096]{1,0:T(8,128)(2,1)} %all-reduce.1) | data formatting | bytes 1048576 | tf_op jit(solution)/shard_map/reshape | solution.py:63
  104.3 2.0 %copy.78 = bf16[32,2,32,32]{2,3,1,0:T(8,128)(2,1)} copy(bf16[32,2,32,32]{3,2,1,0:T(8,128)(2,1)} %param.7) | data formatting | bytes 262144 | tf_op args[3]
  106.4 1.2 slice_negate_fusion
  107.7 0.4 copy-done.1
  108.1 2.7 %fusion.24 = bf16[32,2,128,32]{2,3,1,0:T(8,128)(2,1)} fusion(bf16[32,2,128,32]{3,2,1,0:T(8,128)(2,1)S(1)} %copy-done.1, bf16[32,1,2,32,32]{3,4,1,2,0:T(8,128)(2,1)S(1)} %maximum_bitcast_fusion, bf16[32,1,2,32,32]{3,4,1,2,0:T(8,128)(2,1)} %bitcast.125), kind=kOutput, calls=%fused_computation.40 | convolution fusion | flops 33947648 | bytes 1310720 | tf_op jit(solution)/shard_map/mrpc,mrqco->mqpo/dot_general | solution.py:64
  110.9 2.7 %copy.83 = bf16[32,2,128,32]{3,2,1,0:T(8,128)(2,1)} copy(bf16[32,2,128,32]{2,3,1,0:T(8,128)(2,1)} %fusion.24) | data formatting | bytes 1048576 | tf_op jit(solution)/shard_map/convert_element_type | solution.py:66
  113.5 4.2 %reshape.196 = bf16[64,4096]{1,0:T(8,128)(2,1)} reshape(bf16[32,2,128,32]{3,2,1,0:T(8,128)(2,1)} %copy.83) | data formatting | bytes 1048576 | tf_op jit(solution)/shard_map/reshape | solution.py:67
  118.1 0.3 fusion.93
  118.5 4.1 %collective-permute-start.2 = (bf16[130,1,512]{2,0,1:T(8,128)(2,1)S(1)}, bf16[130,1,512]{2,0,1:T(8,128)(2,1)S(1)}, u32[]{:S(2)}, u32[]{:S(2)}) collective-permute-start(bf16[130,1,512]{2,0,1:T(8,128)(2,1)S(1)} %copy.70), channel_id=1, source_target_pairs={{0,1},{1,2},{2,3},{3,4},{4,5},{5,6},{6,7},{7,8},{8,9},{9,10},{10,1... | collective-permute-start | bytes 399368 | tf_op jit(solution)/shard_map/ppermute | solution.py:17
  122.6 6.4 %collective-permute-start.3 = (bf16[130,1,512]{2,0,1:T(8,128)(2,1)S(1)}, bf16[130,1,512]{2,0,1:T(8,128)(2,1)S(1)}, u32[]{:S(2)}, u32[]{:S(2)}) collective-permute-start(bf16[130,1,512]{2,0,1:T(8,128)(2,1)S(1)} %copy.74), channel_id=1, source_target_pairs={{1,0},{2,1},{3,2},{4,3},{5,4},{6,5},{7,6},{8,7},{9,8},{10,9},{11,1... | collective-permute-start | bytes 399368 | tf_op jit(solution)/shard_map/ppermute | solution.py:19
  129.1 1.7 %fusion.50 = f32[1024,512]{1,0:T(8,128)S(1)} fusion(bf16[1,8,512]{2,1,0:T(8,128)(2,1)S(1)} %collective-permute-done.1, bf16[128,8,512]{2,1,0:T(8,128)(2,1)S(1)} %copy-done, bf16[3,3,512,512]{3,2,1,0:T(8,128)(2,1)} %reshape.184), kind=kOutput, calls=%fused_computation.59 | convolution fusion | flops 537395200 | bytes 3678208 | tf_op jit(solution)/shard_map/dot_general | solution.py:85
  130.8 1.7 %fusion.58 = f32[1024,512]{1,0:T(8,128)S(1)} fusion(bf16[128,8,512]{2,1,0:T(8,128)(2,1)S(1)} %copy-done, bf16[1,8,512]{2,1,0:T(8,128)(2,1)S(1)} %collective-permute-done, bf16[3,3,512,512]{3,2,1,0:T(8,128)(2,1)} %reshape.184), kind=kOutput, calls=%fused_computation.67 | convolution fusion | flops 537395200 | bytes 3678208 | tf_op jit(solution)/shard_map/dot_general | solution.py:85
  132.6 0.2 copy.71
  132.8 0.7 fusion.54
  133.6 0.7 fusion.37
  134.3 0.2 copy.75
  134.5 0.8 fusion.29
  135.3 0.8 fusion.33
  136.0 0.7 fusion.41
  136.8 1.5 %fusion.9 = f32[128,8,512]{2,1,0:T(8,128)S(1)} fusion(f32[1024,512]{1,0:T(8,128)S(1)} %fusion.50, f32[1024,512]{1,0:T(8,128)S(1)} %fusion.54, f32[1024,512]{1,0:T(8,128)S(1)} %fusion.29, f32[512,1024]{0,1:T(8,128)S(1)} %fusion.64, f32[1024,512]{1,0:T(8,128)S(1)} %fusion.37, f32[1024,512]{1,0:T(8,128)S(1)} %fusion.33, f32[1024,512]{1,0:T(8,128)S(1)} %fusion.41, ...), kind=kOutput, calls=%fused_computation.20 | convolution fusion | flops 543162368 | bytes 20729856 | tf_op jit(solution)/shard_map/dot_general | solution.py:85
  138.3 5.6 %fusion.2 = bf16[128,8,512]{2,0,1:T(8,128)(2,1)S(1)} fusion(f32[128,8,512]{2,1,0:T(8,128)S(1)} %fusion.9, f32[512]{0:T(512)S(1)} %add.105, bf16[8,8,8,512]{3,2,1,0:T(8,128)(2,1)S(1)} %bitcast.127, f32[64,128]{1,0:T(8,128)S(1)} %bitcast.130, f32[64]{0:T(128)S(1)} %mul.99), kind=kOutput, calls=%fused_computation.12 | convolution fusion | flops 102252544 | bytes 3705088 | tf_op jit(solution)/shard_map/dot_general | solution.py:94
  143.9 1.5 %copy.86 = bf16[128,8,512]{2,1,0:T(8,128)(2,1)} copy(bf16[128,8,512]{2,0,1:T(8,128)(2,1)S(1)} %fusion.2) | data formatting | bytes 2097152 | tf_op jit(solution)/shard_map/convert_element_type | solution.py:96
  (33 shorter events, 0.7 us)
Async XLA Ops:
  0.7 117.3 %collective-permute-start.1 = (bf16[1,8,512]{2,1,0:T(8,128)(2,1)S(1)}, bf16[1,8,512]{2,1,0:T(8,128)(2,1)S(1)}, u32[]{:S(2)}, u32[]{:S(2)}) collective-permute-start(bf16[1,8,512]{2,1,0:T(8,128)(2,1)S(1)} %get-tuple-element.8), channel_id=1, source_target_pairs={{32,0},{64,32},{96,64},{128,96},{160,128},{192,160},{224,192},{33,... | collective-permute-start | bytes 24584 | tf_op jit(solution)/shard_map/ppermute | solution.py:19
  2.0 116.0 %collective-permute-start = (bf16[1,8,512]{2,1,0:T(8,128)(2,1)S(1)}, bf16[1,8,512]{2,1,0:T(8,128)(2,1)S(1)}, u32[]{:S(2)}, u32[]{:S(2)}) collective-permute-start(bf16[1,8,512]{2,1,0:T(8,128)(2,1)S(1)} %get-tuple-element.7), channel_id=1, source_target_pairs={{0,32},{32,64},{64,96},{96,128},{128,160},{160,192},{192,224},{1,3... | collective-permute-start | bytes 24584 | tf_op jit(solution)/shard_map/ppermute | solution.py:17
  18.8 25.3 %copy-start = (bf16[128,8,512]{2,1,0:T(8,128)(2,1)S(1)}, bf16[128,8,512]{2,1,0:T(8,128)(2,1)}, u32[]{:S(2)}) copy-start(bf16[128,8,512]{2,1,0:T(8,128)(2,1)} %param.4) | copy-start | bytes 3145732
  106.4 1.8 %copy-start.1 = (bf16[32,2,128,32]{3,2,1,0:T(8,128)(2,1)S(1)}, bf16[32,2,128,32]{3,2,1,0:T(8,128)(2,1)}, u32[]{:S(2)}) copy-start(bf16[32,2,128,32]{3,2,1,0:T(8,128)(2,1)} %reshape.195) | copy-start | bytes 1572868
  107.7 3.1 %copy-start.3 = (f32[32]{0:T(128)S(1)}, f32[32]{0:T(128)}, u32[]{:S(2)}) copy-start(f32[32]{0:T(128)} %param.6) | copy-start | bytes 388
  118.4 14.4 %slice-start = ((s8[4718592]{0:T(1024)(128)(4,1)}), s8[4194304]{0:T(1024)(128)(4,1)S(1)}, s32[]{:S(2)}) async-start(s8[4718592]{0:T(1024)(128)(4,1)} %bitcast.123), calls=%async_computation | async-start | bytes 8388608
  118.5 14.1 %collective-permute-start.2 = (bf16[130,1,512]{2,0,1:T(8,128)(2,1)S(1)}, bf16[130,1,512]{2,0,1:T(8,128)(2,1)S(1)}, u32[]{:S(2)}, u32[]{:S(2)}) collective-permute-start(bf16[130,1,512]{2,0,1:T(8,128)(2,1)S(1)} %copy.70), channel_id=1, source_target_pairs={{0,1},{1,2},{2,3},{3,4},{4,5},{5,6},{6,7},{7,8},{8,9},{9,10},{10,1... | collective-permute-start | bytes 399368 | tf_op jit(solution)/shard_map/ppermute | solution.py:17
  122.6 10.2 %slice-start.1 = ((s8[4718592]{0:T(1024)(128)(4,1)}), s8[524288]{0:T(1024)(128)(4,1)S(1)}, s32[]{:S(2)}) async-start(s8[4718592]{0:T(1024)(128)(4,1)} %bitcast.123), calls=%async_computation.1 | async-start | bytes 1048576
  122.6 11.7 %collective-permute-start.3 = (bf16[130,1,512]{2,0,1:T(8,128)(2,1)S(1)}, bf16[130,1,512]{2,0,1:T(8,128)(2,1)S(1)}, u32[]{:S(2)}, u32[]{:S(2)}) collective-permute-start(bf16[130,1,512]{2,0,1:T(8,128)(2,1)S(1)} %copy.74), channel_id=1, source_target_pairs={{1,0},{2,1},{3,2},{4,3},{5,4},{6,5},{7,6},{8,7},{9,8},{10,9},{11,1... | collective-permute-start | bytes 399368 | tf_op jit(solution)/shard_map/ppermute | solution.py:19
  136.8 1.5 %copy-start.2 = (bf16[64,4096]{1,0:T(8,128)(2,1)S(1)}, bf16[64,4096]{1,0:T(8,128)(2,1)}, u32[]{:S(2)}) copy-start(bf16[64,4096]{1,0:T(8,128)(2,1)} %reshape.196) | copy-start | bytes 1572868
where the time goes:
time: 147 us; the launch traced here: 145 us
  blocking collectives  53.2 us (36%)
  local copies, waits for them, and re-layouts  48.8 us (33%)
  matrix products  26.8 us (18%)
  starting transfers between devices  14.8 us (10%)
    psum x1, blocking collectives, shards(): coef = lax.psum(partial_value, 'gx').astype(jnp.bfloat16)  53.2 us
    reshape x1, local copies, waits for them, and re-layouts, band_kernels(): bands.astype(jnp.bfloat16).reshape(3, 3, depth * channels, depth * channels)  25.3 us
    dot_general x9, matrix products, shards(): jnp.dot(window, bands[step_x, step_y], preferred_element_type=jnp.float32)  10.5 us
    ppermute x2, starting transfers between devices, extended(): lax.ppermute(head, axis, [((i + 1) % count, i) for i in range(ends)])  7.72 us
    ppermute x2, starting transfers between devices, extended(): lax.ppermute(tail, axis, [(i, (i + 1) % count) for i in range(ends)])  7.12 us
    convert_element_type x1, local copies, waits for them, and re-layouts, band_kernels(): bands.astype(jnp.bfloat16).reshape(3, 3, depth * channels, depth * channels)  6.88 us
    dot_general x1, matrix products, band_kernels(): jnp.einsum('kzw,abkco->abzcwo', shifts, taps, preferred_element_type=jnp....  6.81 us
    dot_general x1, matrix products, shards(): spectral = jnp.dot(inverse_table, mixed, preferred_element_type=jnp.float32)  5.59 us
  transfers between devices with their start and end apart: 4, of which 0 were waited for; matrix products, arithmetic and copies ran while one was open for 44% of the time, Pallas kernels for 0%

commit v1 on v0

v1 whole, which is shorter than its diff:
```python
import functools
import math

import jax
import jax.numpy as jnp
import numpy as np
from jax import lax
from jax.experimental import pallas as pl
from jax.experimental.pallas import tpu as pltpu
from jax.sharding import PartitionSpec as P

MESH = pl.DeviceIdType.MESH
CHUNKS = 2
F32 = jnp.float32
BF16 = jnp.bfloat16


def dot(a, b):
    return jnp.dot(a, b, preferred_element_type=F32)


def expanded_tables(length, modes, groups, rows_y):
    turns = (np.arange(modes)[:, None] * np.arange(length)[None, :]) % length
    angles = turns.astype(np.float32) * np.float32(2.0 * math.pi / length)
    pairs = np.stack([np.cos(angles), -np.sin(angles)], axis=1) * np.float32(1.0 / math.sqrt(length))
    doubling = np.where(np.arange(modes) == 0, 1.0, 2.0).astype(np.float32)
    forward = pairs.reshape(2 * modes, groups, length // groups).transpose(1, 0, 2)
    inverse = (pairs * doubling[:, None, None]).reshape(2 * modes, groups, length // groups).transpose(1, 2, 0)
    forward = np.repeat(forward, rows_y, axis=2)
    inverse = np.repeat(inverse, rows_y, axis=2)
    return jnp.asarray(forward, BF16), jnp.asarray(inverse, BF16)


def spread(table_ref, out_ref):
    rows, lanes = table_ref.shape

    def body(i, carry):
        part = table_ref[pl.ds(pl.multiple_of(i * 16, 16), 16), :].astype(F32)
        wide = jnp.broadcast_to(part[:, None, :], (16, 8, lanes))
        keep = lax.broadcasted_iota(jnp.int32, (16, 8, lanes), 1) == (
            lax.broadcasted_iota(jnp.int32, (16, 8, lanes), 2) & 7
        )
        out_ref[pl.ds(pl.multiple_of(i * 128, 128), 128), :] = (
            jnp.where(keep, wide, 0.0).reshape(128, lanes).astype(BF16)
        )
        return carry

    lax.fori_loop(0, rows // 16, body, 0)


def layer_kernel(
    field, convw, bias, specw, ftab, itab, out,
    fs, fexp, iexp, cw, sw, bv, amat, gmat, wrep, tmat, cmat, rmat, conv,
    part, cbuf, cland, sbuf, rland, mixed, ybuf, yland, xland, cornl,
    load_sem, bar_send, c_send, c_recv, r_send, r_recv, a_send, a_recv, f_send, f_recv,
    x_send, x_recv, y_send, y_recv, k_send, k_recv,
):
    nch, _, lc = mixed.shape
    tiles = lc // 128
    g = lax.axis_index("gx")
    h = lax.axis_index("gy")
    ng = lax.axis_size("gx")
    nh = lax.axis_size("gy")
    ny = ng // 2
    yc, core = g // 2, g % 2
    q = core * ny + yc
    sib = (2 * yc + (1 - core), h)

    def ychip(j):
        return (2 * lax.rem(yc + j, ny) + core, h)

    left, right = lax.rem(g + ng - 1, ng), lax.rem(g + 1, ng)
    prev, nxt = lax.rem(h + nh - 1, nh), lax.rem(h + 1, nh)
    outer = lax.rem(g + ng + 2 * core - 1, ng)

    def remote(src, dst, s, r, dev):
        return pltpu.make_async_remote_copy(
            src_ref=src, dst_ref=dst, send_sem=s, recv_sem=r, device_id=dev, device_id_type=MESH
        )

    barrier = pltpu.get_barrier_semaphore()
    partners = [sib] + [ychip(j) for j in range(1, ny)] + [(outer, h), (g, prev), (g, nxt)]
    for dev in partners:
        pl.semaphore_signal(barrier, inc=1, device_id=dev, device_id_type=MESH)

    load_f = pltpu.make_async_copy(ftab.at[g], fexp, load_sem.at[0])
    load_x = pltpu.make_async_copy(field, fs.at[1, pl.ds(1, 128)], load_sem.at[1])
    load_i = pltpu.make_async_copy(itab.at[g], iexp, load_sem.at[2])
    load_w = pltpu.make_async_copy(convw, cw, load_sem.at[3])
    load_s = pltpu.make_async_copy(specw.at[pl.ds(4 * q, 4)], sw, load_sem.at[4])
    load_b = pltpu.make_async_copy(bias, bv, load_sem.at[5])
    for load in (load_f, load_x, load_w, load_s, load_i, load_b):
        load.start()

    load_f.wait()
    spread(fexp, amat)
    load_x.wait()
    pl.semaphore_wait(barrier, len(partners))
    x_copies = [
        remote(fs.at[1, pl.ds(127, 2)], xland.at[0], x_send.at[0], x_recv.at[0], (right, h)),
        remote(fs.at[1, pl.ds(1, 2)], xland.at[1], x_send.at[1], x_recv.at[1], (left, h)),
    ]
    for copy in x_copies:
        copy.start()
    c_copies = []
    own_rows = pl.ds(pl.multiple_of(core * 256, 256), 256)
    sib_rows = pl.ds(pl.multiple_of((1 - core) * 256, 256), 256)
    for ch in range(nch):
        cells = fs[1, 1:129, :, ch * lc : (ch + 1) * lc].reshape(1024, lc)
        part[ch] = dot(amat[...], cells)
        cbuf[ch] = part[ch, sib_rows, :].astype(BF16)
        copy = remote(cbuf.at[ch], cland.at[ch], c_send.at[ch], c_recv.at[ch], sib)
        copy.start()
        c_copies.append(copy)

    row = lax.broadcasted_iota(jnp.int32, (64, 256), 0)
    col = lax.broadcasted_iota(jnp.int32, (64, 256), 1)
    pick = jnp.where(col == (row & 31) * 8 + jnp.where(row < 32, 7, 0), 1.0, 0.0).astype(BF16)
    for b in range(4):
        cells = fs[1, 1 + 32 * b : 33 + 32 * b].reshape(256, 512)
        picked = dot(pick, cells).astype(BF16)
        ybuf[0, 32 * b : 32 * b + 32, :] = picked[:32]
        ybuf[1, 32 * b : 32 * b + 32, :] = picked[32:]
    y_copies = [
        remote(ybuf.at[0], yland.at[0], y_send.at[0], y_recv.at[0], (g, nxt)),
        remote(ybuf.at[1], yland.at[1], y_send.at[1], y_recv.at[1], (g, prev)),
    ]
    for copy in y_copies:
        copy.start()

    load_s.wait()
    rep4 = jnp.where(
        (lax.broadcasted_iota(jnp.int32, (32, 128), 1) & 31) == lax.broadcasted_iota(jnp.int32, (32, 128), 0), 1.0, 0.0
    ).astype(BF16)
    sv = dot(sw[...].reshape(256, 32), rep4)
    zlane = lax.broadcasted_iota(jnp.int32, (32, 128), 1) // 32
    for m in range(4):
        wr = sv[m * 64 : m * 64 + 32]
        wi = sv[m * 64 + 32 : m * 64 + 64]
        for r in range(2):
            for z in range(4):
                first = jnp.where(zlane == z, wr if r == 0 else -wi, 0.0)
                second = jnp.where(zlane == z, wi if r == 0 else wr, 0.0)
                rmat[m, r * 128 + z * 32 : r * 128 + z * 32 + 32, :] = jnp.concatenate([first, second], axis=1).astype(BF16)

    load_w.wait()
    rep8 = jnp.where(
        (lax.broadcasted_iota(jnp.int32, (32, 256), 1) & 31) == lax.broadcasted_iota(jnp.int32, (32, 256), 0), 1.0, 0.0
    ).astype(BF16)
    wrep[...] = dot(cw[...].reshape(864, 32), rep8)
    zlane8 = lax.broadcasted_iota(jnp.int32, (32, 256), 1) // 32
    cmat[...] = jnp.zeros_like(cmat)

    def band(t, carry):
        dyi, dxi = t // 3, t % 3
        base = pl.multiple_of((dxi * 3 + dyi) * 96, 32)
        w = [wrep[pl.ds(pl.multiple_of(base + 32 * k, 32), 32), :] for k in range(3)]
        for z in range(8):
            block = jnp.where(zlane8 == z + 1, w[0], 0.0)
            block = jnp.where(zlane8 == z, w[1], block)
            block = jnp.where(zlane8 == z - 1, w[2], block)
            tmat[pl.ds(pl.multiple_of(t * 256 + z * 32, 32), 32), :] = block.astype(BF16)
        cmat[pl.ds(pl.multiple_of(t * 256 + 96, 32), 32), :] = jnp.where(zlane8 == 4, w[0], 0.0).astype(BF16)
        cmat[pl.ds(pl.multiple_of(t * 256 + 128, 32), 32), :] = jnp.where(zlane8 == 3, w[2], 0.0).astype(BF16)
        return carry

    lax.fori_loop(0, 9, band, 0)

    r_copies = []
    for ch in range(nch):
        c_copies[ch].wait_recv()
        total = part[ch, own_rows, :] + cland[ch].astype(F32)
        part[ch, own_rows, :] = total
        sbuf[ch] = total.astype(BF16)
        for j in range(1, ny):
            target = lax.rem(yc + j, ny)
            copy = remote(
                sbuf.at[ch, pl.ds(pl.multiple_of(target * 64, 64), 64)], rland.at[ch, j - 1],
                r_send.at[ch, j - 1], r_recv.at[ch, j - 1], ychip(j),
            )
            copy.start()
            r_copies.append(copy)

    def shift(first, count):
        cells = fs[1, pl.ds(first, count)].astype(F32)
        sub = lax.broadcasted_iota(jnp.int32, cells.shape, 1)
        fs[0, pl.ds(first, count)] = jnp.where(sub == 0, 0.0, pltpu.roll(cells, 1, 1)).astype(BF16)
        fs[2, pl.ds(first, count)] = jnp.where(sub == 7, 0.0, pltpu.roll(cells, 7, 1)).astype(BF16)

    def shift_block(b, carry):
        shift(1 + b * 32, 32)
        return carry

    lax.fori_loop(0, 4, shift_block, 0)
    for copy in x_copies:
        copy.wait()
    has_left = jnp.where(g > 0, 1.0, 0.0)
    has_right = jnp.where(g < ng - 1, 1.0, 0.0)
    k_copies = [
        remote(xland, cornl.at[0], k_send.at[0], k_recv.at[0], (g, nxt)),
        remote(xland, cornl.at[1], k_send.at[1], k_recv.at[1], (g, prev)),
    ]
    for copy in k_copies:
        copy.start()
    fs[1, 0:1] = (xland[0, 1:2].astype(F32) * has_left).astype(BF16)
    fs[1, 129:130] = (xland[1, 0:1].astype(F32) * has_right).astype(BF16)
    shift(0, 1)
    shift(129, 1)

    load_b.wait()
    bias_row = jnp.concatenate([bv[...]] * 16, axis=1)

    def windows(taps, first, count):
        low = jnp.concatenate([t[:, :256] for t in taps], axis=1)
        high = jnp.concatenate([t[:, 256:] for t in taps], axis=1)
        mid = jnp.concatenate([t[:, 128:384] for t in taps], axis=1)
        rows = low.shape[0]
        main = dot(jnp.concatenate([low, high], axis=0), tmat[first : first + count, :])
        cross = dot(mid, cmat[first : first + count, :])
        return jnp.concatenate(
            [
                main[:rows, :128], main[:rows, 128:] + cross[:, :128],
                main[rows:, :128] + cross[:, 128:], main[rows:, 128:],
            ],
            axis=1,
        )

    def conv_block(b, carry):
        taps = [fs[dy, pl.ds(b * 32 + dx, 32)].reshape(256, 512) for dy in range(3) for dx in range(3)]
        value = windows(taps, 0, 2304) + bias_row
        for t in range(4):
            conv[t, pl.ds(pl.multiple_of(b * 256, 256), 256), :] = value[:, 128 * t : 128 * t + 128]
        return carry

    lax.fori_loop(0, 2, conv_block, 0)

    a_copies = []
    f_copies = []
    own_piece = pl.ds(pl.multiple_of(core * 256 + yc * 64, 64), 64)
    mix_rows = pl.ds(pl.multiple_of(q * 64, 64), 64)
    for ch in range(nch):
        coef = part[ch, own_piece, :]
        for j in range(1, ny):
            r_copies[ch * (ny - 1) + j - 1].wait_recv()
            coef = coef + rland[ch, j - 1].astype(F32)
        pieces = []
        for m in range(4):
            rows = jnp.concatenate(
                [
                    jnp.concatenate(
                        [coef[m * 16 + 8 * r : m * 16 + 8 * r + 8, 128 * t : 128 * t + 128] for r in range(2)], axis=1
                    )
                    for t in range(tiles)
                ],
                axis=0,
            ).astype(BF16)
            mix = dot(rows, rmat[m])
            for r in range(2):
                pieces.append(
                    jnp.concatenate([mix[8 * t : 8 * t + 8, 128 * r : 128 * r + 128] for t in range(tiles)], axis=1)
                )
        mixed[ch, mix_rows, :] = jnp.concatenate(pieces, axis=0).astype(BF16)
        block = mixed.at[ch, mix_rows]
        for j in range(1, ny):
            copy = remote(block, block, a_send.at[ch, j - 1], a_recv.at[ch, j - 1], ychip(j))
            copy.start()
            a_copies.append(copy)
        copy = remote(block, block, f_send.at[ch, 0], f_recv.at[ch, 0], sib)
        copy.start()
        f_copies.append(copy)

    lax.fori_loop(2, 4, conv_block, 0)

    row = lax.broadcasted_iota(jnp.int32, (256, 160), 0)
    col = lax.broadcasted_iota(jnp.int32, (256, 160), 1)
    x = row & 127
    for copy in y_copies + k_copies:
        copy.wait()
    for side in range(2):
        yrow = 7 if side == 0 else 0
        inside = jnp.where(row < 128, x - 1, x + 1)
        picks = jnp.where((col == inside) & (col < 128), 1.0, 0.0)
        picks = jnp.where((row == 0) & (col == 128 + 8 + yrow), has_left, picks)
        picks = jnp.where((row == 255) & (col == 128 + 16 + yrow), has_right, picks)
        mid_rows = yland[side]
        source = jnp.concatenate([mid_rows, cornl[side].reshape(32, 512)], axis=0)
        moved = dot(picks.astype(BF16), source).astype(BF16)
        value = windows([moved[:128], mid_rows, moved[128:]], 1536 * side, 768)
        there = (h > 0) if side == 0 else (h < nh - 1)
        value = value * jnp.where(there, 1.0, 0.0)
        edge = pl.ds(0 if side == 0 else 7, 128, stride=8)
        for t in range(4):
            conv[t, edge, :] = conv[t, edge, :] + value[:, 128 * t : 128 * t + 128]

    load_i.wait()
    spread(iexp, gmat)

    for ch in range(nch):
        for j in range(1, ny):
            a_copies[ch * (ny - 1) + j - 1].wait_recv()
            source = core * ny + lax.rem(yc + ny - j, ny)
            block = mixed.at[ch, pl.ds(pl.multiple_of(source * 64, 64), 64)]
            copy = remote(block, block, f_send.at[ch, j], f_recv.at[ch, j], sib)
            copy.start()
            f_copies.append(copy)

    for ch in range(nch):
        for j in range(ny):
            f_copies[ch if j == 0 else nch + ch * (ny - 1) + j - 1].wait_recv()

        def finish(b, carry):
            rows = pl.ds(pl.multiple_of(b * 256, 256), 256)
            lanes = slice(ch * lc, (ch + 1) * lc)
            base = jnp.concatenate([conv[ch * tiles + t, rows, :] for t in range(tiles)], axis=1)
            value = dot(gmat[rows, :], mixed[ch]) + base
            value = 0.5 * value * (1.0 + lax.erf(value * (0.5**0.5)))
            out[pl.ds(b * 32, 32), :, lanes] = value.reshape(32, 8, lc).astype(BF16)
            return carry

        lax.fori_loop(0, 4, finish, 0)

    for copy in c_copies + r_copies + a_copies + f_copies:
        copy.wait_send()


def shards(field, conv_weight, conv_bias, spectral_weight):
    cells_x, cells_y, width = field.shape
    groups = lax.axis_size("gx")
    modes = spectral_weight.shape[0]
    ny = groups // 2
    lc = width // CHUNKS
    ftab, itab = expanded_tables(cells_x * groups, modes, groups, cells_y)
    dma = pltpu.SemaphoreType.DMA
    vmem = pltpu.VMEM
    scratch = [
        vmem((3, cells_x + 2, cells_y, width), BF16),
        vmem((64, 1024), BF16),
        vmem((128, 512), BF16),
        vmem((27, 32, 32), BF16),
        vmem((4, 2, 32, 32), BF16),
        vmem((1, 32), F32),
        vmem((512, 1024), BF16),
        vmem((1024, 512), BF16),
        vmem((864, 256), F32),
        vmem((2304, 256), BF16),
        vmem((2304, 256), BF16),
        vmem((4, 256, 256), BF16),
        vmem((4, 1024, 128), F32),
        vmem((CHUNKS, 512, lc), F32),
        vmem((CHUNKS, 256, lc), BF16),
        vmem((CHUNKS, 256, lc), BF16),
        vmem((CHUNKS, 256, lc), BF16),
        vmem((CHUNKS, ny - 1, 64, lc), BF16),
        vmem((CHUNKS, 512, lc), BF16),
        vmem((2, 128, 512), BF16),
        vmem((2, 128, 512), BF16),
        vmem((2, 2, 8, 512), BF16),
        vmem((2, 2, 2, 8, 512), BF16),
        dma((6,)), dma((1,)),
        dma((CHUNKS,)), dma((CHUNKS,)),
        dma((CHUNKS, ny - 1)), dma((CHUNKS, ny - 1)),
        dma((CHUNKS, ny - 1)), dma((CHUNKS, ny - 1)),
        dma((CHUNKS, ny)), dma((CHUNKS, ny)),
        dma((2,)), dma((2,)), dma((2,)), dma((2,)), dma((2,)), dma((2,)),
    ]
    anywhere = pl.BlockSpec(memory_space=pl.ANY)
    return pl.pallas_call(
        layer_kernel,
        out_shape=jax.ShapeDtypeStruct(field.shape, BF16),
        in_specs=[anywhere] * 6,
        out_specs=pl.BlockSpec(memory_space=pltpu.VMEM),
        scratch_shapes=scratch,
        compiler_params=pltpu.CompilerParams(
            collective_id=0, has_side_effects=True, vmem_limit_bytes=40 * 1024 * 1024
        ),
        name="layer",
    )(field, conv_weight, conv_bias.reshape(1, -1), spectral_weight, ftab, itab)


def solution(mesh):
    placed = (P("gx", "gy", None), P(), P(), P())
    return jax.shard_map(
        shards, mesh=mesh, in_specs=placed, out_specs=P("gx", "gy", None), check_vma=False
    )
```

time: 147 us -> 33.1 us (0.23)
  the two profiles are of different devices: /device:TPU:6 before, /device:TPU:1 now
where the time goes in v1:
time: 33.1 us; the launch traced here: 32.8 us
  Pallas kernels  25.5 us (77%)
  local copies, waits for them, and re-layouts  7.28 us (22%)
    pallas_call x1, Pallas kernels, shards(): pl.pallas_call(layer_kernel, out_shape=jax.ShapeDtypeStruct(field.shape,...  25.5 us
    unnamed x13, local copies, waits for them, and re-layouts  7.28 us

profile of v1, /device:TPU:1, one launch (start us, length us, event | category | flops | bytes accessed | tf_op | source)
XLA Modules:
  0.0 32.8 jit_solution(18427372942402700213)
XLA Ops:
  0.0 0.0 copy-start.5
  0.0 0.7 %copy-done.5 = f32[32]{0:T(128)S(1)} copy-done((f32[32]{0:T(128)S(1)}, f32[32]{0:T(128)}, u32[]{:S(2)}) %copy-start.5) | copy-done | bytes 152
  0.7 0.0 copy-start
  0.7 1.2 %copy-done = bf16[128,8,512]{2,1,0:T(8,128)(2,1)S(1)} copy-done((bf16[128,8,512]{2,1,0:T(8,128)(2,1)S(1)}, bf16[128,8,512]{2,1,0:T(8,128)(2,1)}, u32[]{:S(2)}) %copy-start) | copy-done | bytes 1048600
  1.9 0.0 copy-start.1
  1.9 1.2 %copy-done.1 = bf16[8,128,512]{2,1,0:T(8,128)(2,1)S(1)} copy-done((bf16[8,128,512]{2,1,0:T(8,128)(2,1)S(1)}, bf16[8,128,512]{2,1,0:T(8,128)(2,1)}, u32[]{:S(2)}) %copy-start.1) | copy-done | bytes 1048600
  3.1 0.0 copy-start.2
  3.1 1.2 %copy-done.2 = bf16[8,64,1024]{2,1,0:T(8,128)(2,1)S(1)} copy-done((bf16[8,64,1024]{2,1,0:T(8,128)(2,1)S(1)}, bf16[8,64,1024]{2,1,0:T(8,128)(2,1)}, u32[]{:S(2)}) %copy-start.2) | copy-done | bytes 1048600
  4.3 0.0 copy-start.3
  4.3 1.0 %copy-done.3 = bf16[32,2,32,32]{3,2,1,0:T(8,128)(2,1)S(1)} copy-done((bf16[32,2,32,32]{3,2,1,0:T(8,128)(2,1)S(1)}, bf16[32,2,32,32]{3,2,1,0:T(8,128)(2,1)}, u32[]{:S(2)}) %copy-start.3) | copy-done | bytes 131096
  5.4 0.0 copy-start.4
  5.4 0.9 %copy-done.4 = bf16[27,32,32]{2,1,0:T(8,128)(2,1)S(1)} copy-done((bf16[27,32,32]{2,1,0:T(8,128)(2,1)S(1)}, bf16[27,32,32]{2,1,0:T(8,128)(2,1)}, u32[]{:S(2)}) %copy-start.4) | copy-done | bytes 55320
  6.3 25.5 %layer.1 = bf16[128,8,512]{2,1,0:T(8,128)(2,1)S(1)} custom-call(bf16[128,8,512]{2,1,0:T(8,128)(2,1)S(1)} %copy-done, bf16[27,32,32]{2,1,0:T(8,128)(2,1)S(1)} %copy-done.4, f32[1,32]{1,0:T(1,128)S(1)} %bitcast.1, bf16[32,2,32,32]{3,2,1,0:T(8,128)(2,1)S(1)} %copy-done.3, bf16[8,64,1024]{2,1,0:T(8,128)(2,1)S(1)} %copy-done.2, bf16[8,128,512]{2,1,0:T(8,128)(2,1)S(1)} %copy-done.1), custom_call_target="tpu_custom_call" | custom-call | tf_op jit(solution)/shard_map/layer/pallas_call | solution.py:367
  31.8 1.0 %copy.8 = bf16[128,8,512]{2,1,0:T(8,128)(2,1)} copy(bf16[128,8,512]{2,1,0:T(8,128)(2,1)S(1)} %layer.1) | data formatting | bytes 2097152
Async XLA Ops:
  0.0 0.7 %copy-start.5 = (f32[32]{0:T(128)S(1)}, f32[32]{0:T(128)}, u32[]{:S(2)}) copy-start(f32[32]{0:T(128)} %param.8) | copy-start | bytes 388
  0.7 1.2 %copy-start = (bf16[128,8,512]{2,1,0:T(8,128)(2,1)S(1)}, bf16[128,8,512]{2,1,0:T(8,128)(2,1)}, u32[]{:S(2)}) copy-start(bf16[128,8,512]{2,1,0:T(8,128)(2,1)} %field.1) | copy-start | bytes 3145732
  1.9 1.2 %copy-start.1 = (bf16[8,128,512]{2,1,0:T(8,128)(2,1)S(1)}, bf16[8,128,512]{2,1,0:T(8,128)(2,1)}, u32[]{:S(2)}) copy-start(bf16[8,128,512]{2,1,0:T(8,128)(2,1)} %constant.5.clone.itab) | copy-start | bytes 3145732
  3.1 1.2 %copy-start.2 = (bf16[8,64,1024]{2,1,0:T(8,128)(2,1)S(1)}, bf16[8,64,1024]{2,1,0:T(8,128)(2,1)}, u32[]{:S(2)}) copy-start(bf16[8,64,1024]{2,1,0:T(8,128)(2,1)} %constant.4.clone.ftab) | copy-start | bytes 3145732
  4.3 1.0 %copy-start.3 = (bf16[32,2,32,32]{3,2,1,0:T(8,128)(2,1)S(1)}, bf16[32,2,32,32]{3,2,1,0:T(8,128)(2,1)}, u32[]{:S(2)}) copy-start(bf16[32,2,32,32]{3,2,1,0:T(8,128)(2,1)} %specw.1) | copy-start | bytes 393220
  5.4 0.9 %copy-start.4 = (bf16[27,32,32]{2,1,0:T(8,128)(2,1)S(1)}, bf16[27,32,32]{2,1,0:T(8,128)(2,1)}, u32[]{:S(2)}) copy-start(bf16[27,32,32]{2,1,0:T(8,128)(2,1)} %convw.1) | copy-start | bytes 165892

commit v2 on v1

--- a/solution.py
+++ b/solution.py
@@ -363,18 +363,19 @@
         dma((CHUNKS, ny)), dma((CHUNKS, ny)),
         dma((2,)), dma((2,)), dma((2,)), dma((2,)), dma((2,)), dma((2,)),
     ]
-    anywhere = pl.BlockSpec(memory_space=pl.ANY)
+    operands = (field, conv_weight, conv_bias.reshape(1, -1), spectral_weight, ftab, itab)
+    in_hbm = pl.BlockSpec(memory_space=pltpu.HBM)
     return pl.pallas_call(
         layer_kernel,
         out_shape=jax.ShapeDtypeStruct(field.shape, BF16),
-        in_specs=[anywhere] * 6,
+        in_specs=[in_hbm] * 6,
         out_specs=pl.BlockSpec(memory_space=pltpu.VMEM),
         scratch_shapes=scratch,
         compiler_params=pltpu.CompilerParams(
             collective_id=0, has_side_effects=True, vmem_limit_bytes=40 * 1024 * 1024
         ),
         name="layer",
-    )(field, conv_weight, conv_bias.reshape(1, -1), spectral_weight, ftab, itab)
+    )(*(pltpu.with_memory_space_constraint(a, pltpu.HBM) for a in operands))
 
 
 def solution(mesh):

time: 33.1 us -> 26.6 us (0.80)
  local copies, waits for them, and re-layouts: 7.28 us -> 0.97 us
    unnamed x13 -> x1, local copies, waits for them, and re-layouts: 7.28 us -> 0.97 us
where the time goes in v2:
time: 26.6 us; the launch traced here: 26.5 us
  Pallas kernels  25.5 us (96%)
  local copies, waits for them, and re-layouts  0.97 us (4%)
    pallas_call x1, Pallas kernels, shards(): pl.pallas_call(layer_kernel, out_shape=jax.ShapeDtypeStruct(field.shape,...  25.5 us
    unnamed x1, local copies, waits for them, and re-layouts  0.97 us

profile of v2, /device:TPU:1, one launch (start us, length us, event | category | flops | bytes accessed | tf_op | source)
XLA Modules:
  0.0 26.5 jit_solution(1488131035448435245)
XLA Ops:
  0.0 25.5 %layer.1 = bf16[128,8,512]{2,1,0:T(8,128)(2,1)S(1)} custom-call(bf16[128,8,512]{2,1,0:T(8,128)(2,1)} %field.1, bf16[27,32,32]{2,1,0:T(8,128)(2,1)} %convw.1, f32[1,32]{1,0:T(1,128)} %bitcast.1, bf16[32,2,32,32]{3,2,1,0:T(8,128)(2,1)} %specw.1, bf16[8,64,1024]{2,1,0:T(8,128)(2,1)} %constant.4.clone.ftab, bf16[8,128,512]{2,1,0:T(8,128)(2,1)} %constant.5.clone.itab), custom_call_target="tpu_custom_call" | custom-call | tf_op jit(solution)/shard_map/layer/pallas_call | solution.py:368
  25.5 1.0 %copy.8 = bf16[128,8,512]{2,1,0:T(8,128)(2,1)} copy(bf16[128,8,512]{2,1,0:T(8,128)(2,1)S(1)} %layer.1) | data formatting | bytes 2097152

commit v3 on v2

--- a/solution.py
+++ b/solution.py
@@ -27,7 +27,7 @@
     forward = pairs.reshape(2 * modes, groups, length // groups).transpose(1, 0, 2)
     inverse = (pairs * doubling[:, None, None]).reshape(2 * modes, groups, length // groups).transpose(1, 2, 0)
     forward = np.repeat(forward, rows_y, axis=2)
-    inverse = np.repeat(inverse, rows_y, axis=2)
+    inverse = np.kron(inverse, np.eye(rows_y, dtype=np.float32))
     return jnp.asarray(forward, BF16), jnp.asarray(inverse, BF16)
 
 
@@ -50,10 +50,10 @@
 
 def layer_kernel(
     field, convw, bias, specw, ftab, itab, out,
-    fs, fexp, iexp, cw, sw, bv, amat, gmat, wrep, tmat, cmat, rmat, conv,
+    fs, fexp, cw, sw, bv, amat, gmat, wrep, tmat, cmat, rmat, conv,
     part, cbuf, cland, sbuf, rland, mixed, ybuf, yland, xland, cornl,
     load_sem, bar_send, c_send, c_recv, r_send, r_recv, a_send, a_recv, f_send, f_recv,
-    x_send, x_recv, y_send, y_recv, k_send, k_recv,
+    x_send, x_recv, y_send, y_recv, k_send, k_recv, ready,
 ):
     nch, _, lc = mixed.shape
     tiles = lc // 128
@@ -79,23 +79,81 @@
         )
 
     barrier = pltpu.get_barrier_semaphore()
-    partners = [sib] + [ychip(j) for j in range(1, ny)] + [(outer, h), (g, prev), (g, nxt)]
+    partners = [sib] + [ychip(j) for j in range(1, ny)] + [(outer, h)]
     for dev in partners:
         pl.semaphore_signal(barrier, inc=1, device_id=dev, device_id_type=MESH)
+    first_up = lax.rem(h + 1, 8) != 0
+    first_down = lax.rem(h, 8) == 0
+    has_up, has_down = h < nh - 1, h > 0
+    pairs = [
+        (has_down, first_down, (g, prev), 1),
+        (has_up, first_up, (g, nxt), 0),
+    ]
+    waits = jnp.int32(len(partners))
+    for there, first, dev, _ in pairs:
+
+        @pl.when(there & first)
+        def _(dev=dev):
+            pl.semaphore_signal(barrier, inc=1, device_id=dev, device_id_type=MESH)
+
+        waits = waits + jnp.where(there & ~first, 1, 0)
 
     load_f = pltpu.make_async_copy(ftab.at[g], fexp, load_sem.at[0])
     load_x = pltpu.make_async_copy(field, fs.at[1, pl.ds(1, 128)], load_sem.at[1])
-    load_i = pltpu.make_async_copy(itab.at[g], iexp, load_sem.at[2])
+    load_i = pltpu.make_async_copy(itab.at[g], gmat, load_sem.at[2])
     load_w = pltpu.make_async_copy(convw, cw, load_sem.at[3])
     load_s = pltpu.make_async_copy(specw.at[pl.ds(4 * q, 4)], sw, load_sem.at[4])
     load_b = pltpu.make_async_copy(bias, bv, load_sem.at[5])
-    for load in (load_f, load_x, load_w, load_s, load_i, load_b):
+    for load in (load_f, load_w, load_s, load_x, load_b, load_i):
         load.start()
 
     load_f.wait()
     spread(fexp, amat)
+    load_s.wait()
+    rep4 = jnp.where(
+        (lax.broadcasted_iota(jnp.int32, (32, 128), 1) & 31) == lax.broadcasted_iota(jnp.int32, (32, 128), 0), 1.0, 0.0
+    ).astype(BF16)
+    sv = dot(sw[...].reshape(256, 32), rep4)
+    zlane = lax.broadcasted_iota(jnp.int32, (32, 128), 1) // 32
+    for m in range(4):
+        wr = sv[m * 64 : m * 64 + 32]
+        wi = sv[m * 64 + 32 : m * 64 + 64]
+        for r in range(2):
+            for z in range(4):
+                first = jnp.where(zlane == z, wr if r == 0 else -wi, 0.0)
+                second = jnp.where(zlane == z, wi if r == 0 else wr, 0.0)
+                rmat[m, r * 128 + z * 32 : r * 128 + z * 32 + 32, :] = jnp.concatenate([first, second], axis=1).astype(BF16)
+
+    load_w.wait()
+    rep8 = jnp.where(
+        (lax.broadcasted_iota(jnp.int32, (32, 256), 1) & 31) == lax.broadcasted_iota(jnp.int32, (32, 256), 0), 1.0, 0.0
+    ).astype(BF16)
+    wrep[...] = dot(cw[...].reshape(864, 32), rep8)
+    zlane8 = lax.broadcasted_iota(jnp.int32, (32, 256), 1) // 32
+    cmat[...] = jnp.zeros_like(cmat)
+
+    def band(t, carry):
+        dyi, dxi = t // 3, t % 3
+        base = pl.multiple_of((dxi * 3 + dyi) * 96, 32)
+        w = [wrep[pl.ds(pl.multiple_of(base + 32 * k, 32), 32), :] for k in range(3)]
+        for z in range(8):
+            block = jnp.where(zlane8 == z + 1, w[0], 0.0)
+            block = jnp.where(zlane8 == z, w[1], block)
+            block = jnp.where(zlane8 == z - 1, w[2], block)
+            tmat[pl.ds(pl.multiple_of(t * 256 + z * 32, 32), 32), :] = block.astype(BF16)
+        cmat[pl.ds(pl.multiple_of(t * 256 + 96, 32), 32), :] = jnp.where(zlane8 == 4, w[0], 0.0).astype(BF16)
+        cmat[pl.ds(pl.multiple_of(t * 256 + 128, 32), 32), :] = jnp.where(zlane8 == 3, w[2], 0.0).astype(BF16)
+        return carry
+
+    lax.fori_loop(0, 4, band, 0)
     load_x.wait()
-    pl.semaphore_wait(barrier, len(partners))
+    pl.semaphore_wait(barrier, waits)
+    for there, first, dev, lands in pairs:
+
+        @pl.when(there & ~first)
+        def _(dev=dev, lands=lands):
+            pl.semaphore_signal(ready.at[lands], inc=1, device_id=dev, device_id_type=MESH)
+
     x_copies = [
         remote(fs.at[1, pl.ds(127, 2)], xland.at[0], x_send.at[0], x_recv.at[0], (right, h)),
         remote(fs.at[1, pl.ds(1, 2)], xland.at[1], x_send.at[1], x_recv.at[1], (left, h)),
@@ -122,49 +180,17 @@
         ybuf[0, 32 * b : 32 * b + 32, :] = picked[:32]
         ybuf[1, 32 * b : 32 * b + 32, :] = picked[32:]
     y_copies = [
+        remote(ybuf.at[1], yland.at[1], y_send.at[1], y_recv.at[1], (g, prev)),
         remote(ybuf.at[0], yland.at[0], y_send.at[0], y_recv.at[0], (g, nxt)),
-        remote(ybuf.at[1], yland.at[1], y_send.at[1], y_recv.at[1], (g, prev)),
     ]
-    for copy in y_copies:
-        copy.start()
-
-    load_s.wait()
-    rep4 = jnp.where(
-        (lax.broadcasted_iota(jnp.int32, (32, 128), 1) & 31) == lax.broadcasted_iota(jnp.int32, (32, 128), 0), 1.0, 0.0
-    ).astype(BF16)
-    sv = dot(sw[...].reshape(256, 32), rep4)
-    zlane = lax.broadcasted_iota(jnp.int32, (32, 128), 1) // 32
-    for m in range(4):
-        wr = sv[m * 64 : m * 64 + 32]
-        wi = sv[m * 64 + 32 : m * 64 + 64]
-        for r in range(2):
-            for z in range(4):
-                first = jnp.where(zlane == z, wr if r == 0 else -wi, 0.0)
-                second = jnp.where(zlane == z, wi if r == 0 else wr, 0.0)
-                rmat[m, r * 128 + z * 32 : r * 128 + z * 32 + 32, :] = jnp.concatenate([first, second], axis=1).astype(BF16)
-
-    load_w.wait()
-    rep8 = jnp.where(
-        (lax.broadcasted_iota(jnp.int32, (32, 256), 1) & 31) == lax.broadcasted_iota(jnp.int32, (32, 256), 0), 1.0, 0.0
-    ).astype(BF16)
-    wrep[...] = dot(cw[...].reshape(864, 32), rep8)
-    zlane8 = lax.broadcasted_iota(jnp.int32, (32, 256), 1) // 32
-    cmat[...] = jnp.zeros_like(cmat)
-
-    def band(t, carry):
-        dyi, dxi = t // 3, t % 3
-        base = pl.multiple_of((dxi * 3 + dyi) * 96, 32)
-        w = [wrep[pl.ds(pl.multiple_of(base + 32 * k, 32), 32), :] for k in range(3)]
-        for z in range(8):
-            block = jnp.where(zlane8 == z + 1, w[0], 0.0)
-            block = jnp.where(zlane8 == z, w[1], block)
-            block = jnp.where(zlane8 == z - 1, w[2], block)
-            tmat[pl.ds(pl.multiple_of(t * 256 + z * 32, 32), 32), :] = block.astype(BF16)
-        cmat[pl.ds(pl.multiple_of(t * 256 + 96, 32), 32), :] = jnp.where(zlane8 == 4, w[0], 0.0).astype(BF16)
-        cmat[pl.ds(pl.multiple_of(t * 256 + 128, 32), 32), :] = jnp.where(zlane8 == 3, w[2], 0.0).astype(BF16)
-        return carry
-
-    lax.fori_loop(0, 9, band, 0)
+    k_copies = [
+        remote(xland, cornl.at[1], k_send.at[1], k_recv.at[1], (g, prev)),
+        remote(xland, cornl.at[0], k_send.at[0], k_recv.at[0], (g, nxt)),
+    ]
+    for (there, first, _, _), copy in zip(pairs, y_copies):
+        pl.when(there & ~first)(copy.start)
+
+    lax.fori_loop(4, 9, band, 0)
 
     r_copies = []
     for ch in range(nch):
@@ -196,12 +222,8 @@
         copy.wait()
     has_left = jnp.where(g > 0, 1.0, 0.0)
     has_right = jnp.where(g < ng - 1, 1.0, 0.0)
-    k_copies = [
-        remote(xland, cornl.at[0], k_send.at[0], k_recv.at[0], (g, nxt)),
-        remote(xland, cornl.at[1], k_send.at[1], k_recv.at[1], (g, prev)),
-    ]
-    for copy in k_copies:
-        copy.start()
+    for (there, first, _, _), copy in zip(pairs, k_copies):
+        pl.when(there & ~first)(copy.start)
     fs[1, 0:1] = (xland[0, 1:2].astype(F32) * has_left).astype(BF16)
     fs[1, 129:130] = (xland[1, 0:1].astype(F32) * has_right).astype(BF16)
     shift(0, 1)
@@ -269,31 +291,37 @@
         copy.start()
         f_copies.append(copy)
 
+    for (there, first, _, lands), y_copy, k_copy in zip(pairs, y_copies, k_copies):
+
+        @pl.when(there & first)
+        def _(lands=lands, y_copy=y_copy, k_copy=k_copy):
+            pl.semaphore_wait(ready.at[1 - lands], 1)
+            y_copy.start()
+            k_copy.start()
+
     lax.fori_loop(2, 4, conv_block, 0)
 
     row = lax.broadcasted_iota(jnp.int32, (256, 160), 0)
     col = lax.broadcasted_iota(jnp.int32, (256, 160), 1)
     x = row & 127
-    for copy in y_copies + k_copies:
-        copy.wait()
     for side in range(2):
-        yrow = 7 if side == 0 else 0
-        inside = jnp.where(row < 128, x - 1, x + 1)
-        picks = jnp.where((col == inside) & (col < 128), 1.0, 0.0)
-        picks = jnp.where((row == 0) & (col == 128 + 8 + yrow), has_left, picks)
-        picks = jnp.where((row == 255) & (col == 128 + 16 + yrow), has_right, picks)
-        mid_rows = yland[side]
-        source = jnp.concatenate([mid_rows, cornl[side].reshape(32, 512)], axis=0)
-        moved = dot(picks.astype(BF16), source).astype(BF16)
-        value = windows([moved[:128], mid_rows, moved[128:]], 1536 * side, 768)
-        there = (h > 0) if side == 0 else (h < nh - 1)
-        value = value * jnp.where(there, 1.0, 0.0)
-        edge = pl.ds(0 if side == 0 else 7, 128, stride=8)
-        for t in range(4):
-            conv[t, edge, :] = conv[t, edge, :] + value[:, 128 * t : 128 * t + 128]
-
-    load_i.wait()
-    spread(iexp, gmat)
+
+        @pl.when(pairs[side][0])
+        def _(side=side):
+            y_copies[1 - side].wait_recv()
+            k_copies[1 - side].wait_recv()
+            yrow = 7 if side == 0 else 0
+            inside = jnp.where(row < 128, x - 1, x + 1)
+            picks = jnp.where((col == inside) & (col < 128), 1.0, 0.0)
+            picks = jnp.where((row == 0) & (col == 128 + 8 + yrow), has_left, picks)
+            picks = jnp.where((row == 255) & (col == 128 + 16 + yrow), has_right, picks)
+            mid_rows = yland[side]
+            source = jnp.concatenate([mid_rows, cornl[side].reshape(32, 512)], axis=0)
+            moved = dot(picks.astype(BF16), source).astype(BF16)
+            value = windows([moved[:128], mid_rows, moved[128:]], 1536 * side, 768)
+            edge = pl.ds(0 if side == 0 else 7, 128, stride=8)
+            for t in range(4):
+                conv[t, edge, :] = conv[t, edge, :] + value[:, 128 * t : 128 * t + 128]
 
     for ch in range(nch):
         for j in range(1, ny):
@@ -304,6 +332,7 @@
             copy.start()
             f_copies.append(copy)
 
+    load_i.wait()
     for ch in range(nch):
         for j in range(ny):
             f_copies[ch if j == 0 else nch + ch * (ny - 1) + j - 1].wait_recv()
@@ -321,6 +350,12 @@
 
     for copy in c_copies + r_copies + a_copies + f_copies:
         copy.wait_send()
+    for (there, _, _, _), y_copy, k_copy in zip(pairs, y_copies, k_copies):
+
+        @pl.when(there)
+        def _(y_copy=y_copy, k_copy=k_copy):
+            y_copy.wait_send()
+            k_copy.wait_send()
 
 
 def shards(field, conv_weight, conv_bias, spectral_weight):
@@ -335,7 +370,6 @@
     scratch = [
         vmem((3, cells_x + 2, cells_y, width), BF16),
         vmem((64, 1024), BF16),
-        vmem((128, 512), BF16),
         vmem((27, 32, 32), BF16),
         vmem((4, 2, 32, 32), BF16),
         vmem((1, 32), F32),
@@ -362,6 +396,7 @@
         dma((CHUNKS, ny - 1)), dma((CHUNKS, ny - 1)),
         dma((CHUNKS, ny)), dma((CHUNKS, ny)),
         dma((2,)), dma((2,)), dma((2,)), dma((2,)), dma((2,)), dma((2,)),
+        pltpu.SemaphoreType.REGULAR((2,)),
     ]
     operands = (field, conv_weight, conv_bias.reshape(1, -1), spectral_weight, ftab, itab)
     in_hbm = pl.BlockSpec(memory_space=pltpu.HBM)

time: 26.6 us -> 22.1 us (0.83)
  the two profiles are of different devices: /device:TPU:1 before, /device:TPU:165 now
where the time goes in v3:
time: 22.1 us; the launch traced here: 22 us
  Pallas kernels  21 us (95%)
  local copies, waits for them, and re-layouts  0.97 us (4%)
    pallas_call x1, Pallas kernels, shards(): pl.pallas_call(layer_kernel, out_shape=jax.ShapeDtypeStruct(field.shape,...  21 us
    unnamed x1, local copies, waits for them, and re-layouts  0.97 us

profile of v3, /device:TPU:165, one launch (start us, length us, event | category | flops | bytes accessed | tf_op | source)
XLA Modules:
  0.0 22.0 jit_solution(4951905211295561484)
XLA Ops:
  0.0 21.0 %layer.1 = bf16[128,8,512]{2,1,0:T(8,128)(2,1)S(1)} custom-call(bf16[128,8,512]{2,1,0:T(8,128)(2,1)} %field.1, bf16[27,32,32]{2,1,0:T(8,128)(2,1)} %convw.1, f32[1,32]{1,0:T(1,128)} %bitcast.1, bf16[32,2,32,32]{3,2,1,0:T(8,128)(2,1)} %specw.1, bf16[8,64,1024]{2,1,0:T(8,128)(2,1)} %constant.4.clone.ftab, bf16[8,1024,512]{2,1,0:T(8,128)(2,1)} %constant.5.clone.itab), custom_call_target="tpu_custom_call" | custom-call | tf_op jit(solution)/shard_map/layer/pallas_call | solution.py:403
  21.0 1.0 %copy.8 = bf16[128,8,512]{2,1,0:T(8,128)(2,1)} copy(bf16[128,8,512]{2,1,0:T(8,128)(2,1)S(1)} %layer.1) | data formatting | bytes 2097152
